TPU v7x, 32 devices: a whole 2x2x4 slice. The times are simulated.
32 devices in a mesh: scene: 2 (over y), lines: 16 (over z, x, core).
Axes of the slice: x: 2, y: 2, z: 4, core: 2. Of those that a mesh axis runs over, the one named last changes fastest.
Arguments:
- pixels: bfloat16 [1024, 128, 256], P(('scene', 'lines')), parts along dimension 0, may hold values from -100 to 100
- scene_lines: int32 [2], P('scene'), parts along dimension 0, may hold values from 385 to 512
- scene_cols: int32 [2], P('scene'), parts along dimension 0, may hold values from 33 to 128
Outputs:
- anomaly: float32 [1024, 128], P(('scene', 'lines')), parts along dimension 0
There are 2 independent parts, one for each index of `scene`. A program takes and returns all parts, laid end to end along the dimension named above; each array names one. Nothing has to cross between parts.
Inputs may be any that keep to these rules, and one draw needn't show every extreme that they name: The scene occupies the first scene_lines lines of the array. The scene occupies the first scene_cols columns of every line.
All inputs are finite; a program needn't handle non-finite values.
Results may differ from a plain program's by a relative error of at most 0.0003.
Values may be sent and summed in bfloat16 or wider, within the bound.
A program may use at most 64 MiB of HBM per device.

v0:
```python
import functools

import jax
import jax.numpy as jnp
from jax import lax
from jax.experimental import pallas as pl
from jax.experimental.pallas import tpu as pltpu
from jax.sharding import PartitionSpec as P

OUTER = 32
GUARD = 4
SLAB = 32
HIGHEST = lax.Precision.HIGHEST
MESH = pl.DeviceIdType.MESH
BF16 = jnp.bfloat16
F32 = jnp.float32
TN = (((0,), (0,)), ((), ()))
NT = (((1,), (1,)), ((), ()))


def iota(shape, dim):
    return lax.broadcasted_iota(jnp.int32, shape, dim)


def split(value):
    high = value.astype(BF16)
    return high, (value - high.astype(F32)).astype(BF16)


def gram_kernel(info, x_ref, out_ref, gram, sums):
    lines, cols, bands = x_ref.shape
    first, last_line, last_col = info[0], info[1], info[2]
    col_ok = iota((cols, bands), 0) < last_col
    gram[...] = jnp.zeros_like(gram)
    sums[...] = jnp.zeros_like(sums)
    step = 4

    def add(i, _):
        rows = []
        for j in range(step):
            line = i * step + j
            ok = col_ok & (first + line < last_line)
            rows.append(jnp.where(ok, x_ref[line].astype(F32), 0.0).astype(BF16))
        block = jnp.concatenate(rows, axis=0)
        gram[...] += lax.dot_general(block, block, TN, preferred_element_type=F32)
        ones = jnp.ones((8, step * cols), BF16)
        sums[...] += jnp.dot(ones, block, preferred_element_type=F32)
        return 0

    lax.fori_loop(0, lines // step, add, 0)
    h = bands // 2
    out_ref[0:h] = gram[:h, :h]
    out_ref[h : 2 * h] = gram[:h, h:]
    out_ref[2 * h : 3 * h] = gram[h:, h:]
    out_ref[3 * h :] = jnp.zeros((h, h), F32)
    out_ref[3 * h : 3 * h + 8] = sums[:, :h]
    out_ref[3 * h + 8 : 3 * h + 16] = sums[:, h:]


def reduce_kernel(n, g_ref, out_ref, recv, s1, r1, s2, r2):
    me = lax.axis_index("lines")
    bar = pltpu.get_barrier_semaphore()

    def greet(d, _):
        pl.semaphore_signal(bar, inc=1, device_id={"lines": lax.rem(me + d, n)}, device_id_type=MESH)
        return 0

    lax.fori_loop(1, n, greet, 0)
    pl.semaphore_wait(bar, n - 1)

    def scatter(d):
        peer = lax.rem(me + d, n)
        return pltpu.make_async_remote_copy(
            src_ref=g_ref.at[peer], dst_ref=recv.at[me], send_sem=s1.at[d], recv_sem=r1.at[d],
            device_id={"lines": peer}, device_id_type=MESH)

    def gather(d):
        peer = lax.rem(me + d, n)
        return pltpu.make_async_remote_copy(
            src_ref=out_ref.at[me], dst_ref=out_ref.at[me], send_sem=s2.at[d], recv_sem=r2.at[d],
            device_id={"lines": peer}, device_id_type=MESH)

    def start1(d, _):
        scatter(d).start()
        return 0

    lax.fori_loop(1, n, start1, 0)

    def take(d, total):
        source = lax.rem(me + n - d, n)
        pltpu.make_async_remote_copy(
            src_ref=g_ref.at[source], dst_ref=recv.at[source], send_sem=s1.at[d], recv_sem=r1.at[d],
            device_id={"lines": source}, device_id_type=MESH).wait_recv()
        return total + recv[source]

    out_ref[me] = lax.fori_loop(1, n, take, g_ref[me])

    def start2(d, _):
        gather(d).start()
        return 0

    lax.fori_loop(1, n, start2, 0)

    def finish(d, _):
        source = lax.rem(me + n - d, n)
        pltpu.make_async_remote_copy(
            src_ref=out_ref.at[source], dst_ref=out_ref.at[source], send_sem=s2.at[d], recv_sem=r2.at[d],
            device_id={"lines": source}, device_id_type=MESH).wait_recv()
        scatter(d).wait_send()
        gather(d).wait_send()
        return 0

    lax.fori_loop(1, n, finish, 0)


def whiten_kernel(info, g_ref, high_ref, low_ref, mat):
    h = g_ref.shape[1]
    bands = 2 * h
    total = (info[1] * info[2]).astype(F32)
    sums = jnp.concatenate([g_ref[3 * h : 3 * h + 8], g_ref[3 * h + 8 : 3 * h + 16]], axis=1)
    sums = jnp.where(iota((8, bands), 0) == 0, sums, 0.0)
    outer = lax.dot_general(sums, sums, TN, precision=HIGHEST, preferred_element_type=F32)
    scale = total - 1.0
    mat[:h, :h] = (g_ref[0:h] - outer[:h, :h] / total) / scale
    mat[:h, h:] = (g_ref[h : 2 * h] - outer[:h, h:] / total) / scale
    mat[h:, h:] = (g_ref[2 * h : 3 * h] - outer[h:, h:] / total) / scale
    mat[h:, :h] = jnp.zeros((h, h), F32)
    lane = iota((SLAB, bands), 1)
    row = iota((SLAB, bands), 0)
    for base in range(0, bands, SLAB):
        slab = mat[base : base + SLAB, :]
        pivots = jnp.ones((SLAB, bands), F32)
        for j in range(SLAB):
            k = base + j
            column = jnp.broadcast_to(slab[:, k : k + 1], (SLAB, bands))
            pivot = jnp.broadcast_to(column[j : j + 1, :], (SLAB, bands))
            pivots = jnp.where(row == j, pivot, pivots)
            factor = jnp.where(row > j, column / pivot, 0.0)
            line = jnp.broadcast_to(slab[j : j + 1, :], (SLAB, bands))
            line = jnp.where(lane == k, 1.0, line)
            slab = jnp.where((lane == k) & (row > j), 0.0, slab) - factor * line
        inside = (lane >= base) & (lane < base + SLAB)
        unit = jnp.where(lane == base + row, 1.0, jnp.where(inside & (lane > base + row), 0.0, slab))
        below = jnp.where(lane < base + SLAB, unit, 0.0)
        high, low = split(below * lax.rsqrt(pivots))
        high_ref[base : base + SLAB, :] = high
        low_ref[base : base + SLAB, :] = low
        rest = bands - base - SLAB
        if rest:
            update = lax.dot_general(
                slab, unit / pivots, TN, precision=HIGHEST, preferred_element_type=F32)
            old = mat[base + SLAB :, :]
            wide = iota((rest, bands), 1)
            cleared = jnp.where((wide >= base) & (wide < base + SLAB), 0.0, old)
            mat[base + SLAB :, :] = cleared - update[base + SLAB :, :]


def score_kernel(info, x_ref, before_ref, after_ref, high_ref, low_ref, out_ref, ext, outer, guard):
    lines, cols, bands = x_ref.shape
    first, last_line, last_col = info[0], info[1], info[2]
    col_ok = iota((cols, bands), 0) < last_col

    def mask(i, _):
        for part, ref in enumerate((before_ref, x_ref, after_ref)):
            line = first + (part - 1) * lines + i
            ok = col_ok & (line >= 0) & (line < last_line)
            ext[part * lines + i] = jnp.where(ok, ref[i].astype(F32), 0.0).astype(BF16)
        return 0

    lax.fori_loop(0, lines, mask, 0)

    def total(lo, hi):
        def add(i, acc):
            return acc + ext[i].astype(F32)
        return lax.fori_loop(lo, hi, add, jnp.zeros((cols, bands), F32))

    outer[...] = total(lines - OUTER, lines + OUTER)
    guard[...] = total(lines - GUARD, lines + GUARD)
    gap = jnp.abs(iota((cols, cols), 0) - iota((cols, cols), 1))
    near = jnp.where(gap <= OUTER, 1.0, 0.0).astype(BF16)
    close = jnp.where(gap <= GUARD, -1.0, 0.0).astype(BF16)
    windows = jnp.concatenate([near, near, close, close], axis=1)
    col = iota((cols, bands), 0)

    def span(place, end, radius):
        return jnp.maximum(jnp.minimum(place + radius, end - 1) - jnp.maximum(place - radius, 0) + 1, 0)

    outer_cols = span(col, last_col, OUTER).astype(F32)
    guard_cols = span(col, last_col, GUARD).astype(F32)
    step = 2

    def score(i, _):
        highs, lows = [], []
        for j in range(step):
            line = i * step + j
            at = lines + line
            wide = outer[...] + ext[at + OUTER].astype(F32)
            tight = guard[...] + ext[at + GUARD].astype(F32)
            stack = jnp.concatenate(split(wide) + split(tight), axis=0)
            outer[...] = wide - ext[at - OUTER].astype(F32)
            guard[...] = tight - ext[at - GUARD].astype(F32)
            cycle = jnp.dot(windows, stack, preferred_element_type=F32)
            place = first + line
            count = (span(place, last_line, OUTER).astype(F32) * outer_cols
                     - span(place, last_line, GUARD).astype(F32) * guard_cols)
            deviation = x_ref[line].astype(F32) - cycle / jnp.maximum(count, 1.0)
            high, low = split(deviation)
            highs.append(high)
            lows.append(low)
        high = jnp.concatenate(highs, axis=0)
        low = jnp.concatenate(lows, axis=0)
        white = lax.dot_general(high_ref[...], high, NT, preferred_element_type=F32)
        white += lax.dot_general(high_ref[...], low, NT, preferred_element_type=F32)
        white += lax.dot_general(low_ref[...], high, NT, preferred_element_type=F32)
        power = jnp.sum(white * white, axis=0, keepdims=True) / bands
        for j in range(step):
            line = i * step + j
            ok = (iota((1, cols), 1) < last_col) & (first + line < last_line)
            out_ref[pl.ds(line, 1), :] = jnp.where(ok, power[:, j * cols : (j + 1) * cols], 0.0)
        return 0

    lax.fori_loop(0, lines // step, score, 0)


VMEM = pl.BlockSpec(memory_space=pltpu.VMEM)
SMEM = pl.BlockSpec(memory_space=pltpu.SMEM)


def call(kernel, out_shape, specs, scratch, limit, flops, moved, **params):
    return pl.pallas_call(
        kernel, out_shape=out_shape, in_specs=specs,
        out_specs=jax.tree.map(lambda _: VMEM, out_shape), scratch_shapes=scratch,
        compiler_params=pltpu.CompilerParams(vmem_limit_bytes=limit << 20, **params),
        cost_estimate=pl.CostEstimate(flops=flops, bytes_accessed=moved, transcendentals=0))


def body(pixels, scene_lines, scene_cols):
    lines, cols, bands = pixels.shape
    n = lax.axis_size("lines")
    first = lax.axis_index("lines") * lines
    info = jnp.concatenate([first[None].astype(jnp.int32), scene_lines, scene_cols])
    before = lax.ppermute(pixels, "lines", [(i, i + 1) for i in range(n - 1)])
    after = lax.ppermute(pixels, "lines", [(i + 1, i) for i in range(n - 1)])
    half = bands // 2
    gram = call(
        gram_kernel, jax.ShapeDtypeStruct((4 * half, half), F32), [SMEM, VMEM],
        [pltpu.VMEM((bands, bands), F32), pltpu.VMEM((8, bands), F32)], 16,
        4000000000, pixels.size * 2)(info, pixels)
    gram = gram.reshape(n, 4 * half // n, half)
    sems = [pltpu.SemaphoreType.DMA((n,))] * 4
    gram = call(
        functools.partial(reduce_kernel, n), jax.ShapeDtypeStruct(gram.shape, F32), [VMEM],
        [pltpu.VMEM(gram.shape, F32)] + sems, 16, 4000000000, 40000000,
        collective_id=0, has_side_effects=True)(gram)
    gram = gram.reshape(4 * half, half)
    shape = jax.ShapeDtypeStruct((bands, bands), BF16)
    high, low = call(
        whiten_kernel, [shape, shape], [SMEM, VMEM], [pltpu.VMEM((bands, bands), F32)], 16,
        10000000000, 60000000)(info, gram)
    return call(
        score_kernel, jax.ShapeDtypeStruct((lines, cols), F32), [SMEM] + [VMEM] * 5,
        [pltpu.VMEM((lines + 2 * OUTER, cols, bands), BF16)] + [pltpu.VMEM((cols, bands), F32)] * 2, 40,
        8000000000, 8000000)(info, pixels, before, after, high, low)


def solution(mesh):
    in_specs = (P(("scene", "lines"), None, None), P("scene"), P("scene"))
    out_specs = P(("scene", "lines"), None)
    return jax.shard_map(body, mesh=mesh, in_specs=in_specs, out_specs=out_specs, check_vma=False)
```

profile of v0, /device:TPU:29, one launch (start us, length us, event | category | flops | bytes accessed | tf_op | source)
XLA Modules:
  0.0 113.8 jit_solution(16864958773619274571)
XLA Ops:
  0.0 2.6 %collective-permute-start.1 = (bf16[32,128,256]{2,1,0:T(8,128)(2,1)}, bf16[32,128,256]{2,1,0:T(8,128)(2,1)S(1)}, u32[]{:S(2)}, u32[]{:S(2)}) collective-permute-start(bf16[32,128,256]{2,1,0:T(8,128)(2,1)} %x_ref.3), channel_id=1, source_target_pairs={{1,0},{2,1},{3,2},{4,3},{5,4},{6,5},{7,6},{8,7},{9,8},{10,9},{11,1... | collective-permute-start | bytes 6291464 | tf_op jit(solution)/shard_map/ppermute | solution.py:243
  2.6 3.0 %collective-permute-start = (bf16[32,128,256]{2,1,0:T(8,128)(2,1)}, bf16[32,128,256]{2,1,0:T(8,128)(2,1)}, u32[]{:S(2)}, u32[]{:S(2)}) collective-permute-start(bf16[32,128,256]{2,1,0:T(8,128)(2,1)} %x_ref.3), channel_id=1, source_target_pairs={{0,1},{1,2},{2,3},{3,4},{4,5},{5,6},{6,7},{7,8},{8,9},{9,10},{10,1... | collective-permute-start | bytes 6291464 | tf_op jit(solution)/shard_map/ppermute | solution.py:242
  6.9 0.1 pad_add_fusion.info
  7.0 0.0 copy-start
  7.0 1.6 %copy-done = bf16[32,128,256]{2,1,0:T(8,128)(2,1)S(1)} copy-done((bf16[32,128,256]{2,1,0:T(8,128)(2,1)S(1)}, bf16[32,128,256]{2,1,0:T(8,128)(2,1)}, u32[]{:S(2)}) %copy-start) | copy-done | bytes 2097176
  8.6 3.2 %shard_map.37 = f32[512,128]{1,0:T(8,128)S(1)} custom-call(s32[3]{0:T(128)S(1)} %pad_add_fusion.info, bf16[32,128,256]{2,1,0:T(8,128)(2,1)S(1)} %copy-done), custom_call_target="tpu_custom_call" | custom-call | flops 4000000000 | bytes 2097152 | tf_op jit(solution)/shard_map/pallas_call | solution.py:245
  11.8 50.8 %shard_map.38 = f32[16,32,128]{2,1,0:T(8,128)S(1)} custom-call(f32[16,32,128]{2,1,0:T(8,128)S(1)} %bitcast.4), custom_call_target="tpu_custom_call" | custom-call | flops 4000000000 | bytes 40000000 | tf_op jit(solution)/shard_map/pallas_call | solution.py:251
  62.5 0.0 copy-start.1
  62.6 36.2 %shard_map.39 = (bf16[256,256]{1,0:T(8,128)(2,1)S(1)}, bf16[256,256]{1,0:T(8,128)(2,1)S(1)}) custom-call(s32[3]{0:T(128)S(1)} %pad_add_fusion.info, f32[512,128]{1,0:T(8,128)S(1)} %bitcast.3), custom_call_target="tpu_custom_call" | custom-call | flops 10000000000 | bytes 60000000 | tf_op jit(solution)/shard_map/pallas_call | solution.py:257
  98.8 0.0 collective-permute-done.1.after_ref
  98.8 0.0 collective-permute-done.before_ref
  98.8 0.0 copy-done.1
  98.8 14.9 %shard_map.40 = f32[32,128]{1,0:T(8,128)} custom-call(s32[3]{0:T(128)S(1)} %pad_add_fusion.info, bf16[32,128,256]{2,1,0:T(8,128)(2,1)S(1)} %copy-done.1, bf16[32,128,256]{2,1,0:T(8,128)(2,1)} %collective-permute-done.before_ref, bf16[32,128,256]{2,1,0:T(8,128)(2,1)S(1)} %collective-permute-done.1.after_ref, bf16[256,256]{1,0:T(8,128)(2,1)S(1)} %get-tuple-element.7.high_ref, ...), custom_call_target="tpu_custom_call" | custom-call | flops 8000000000 | bytes 8000000 | tf_op jit(solution)/shard_map/pallas_call | solution.py:260
Async XLA Ops:
  0.0 98.8 %collective-permute-start.1 = (bf16[32,128,256]{2,1,0:T(8,128)(2,1)}, bf16[32,128,256]{2,1,0:T(8,128)(2,1)S(1)}, u32[]{:S(2)}, u32[]{:S(2)}) collective-permute-start(bf16[32,128,256]{2,1,0:T(8,128)(2,1)} %x_ref.3), channel_id=1, source_target_pairs={{1,0},{2,1},{3,2},{4,3},{5,4},{6,5},{7,6},{8,7},{9,8},{10,9},{11,1... | collective-permute-start | bytes 6291464 | tf_op jit(solution)/shard_map/ppermute | solution.py:243
  2.6 96.2 %collective-permute-start = (bf16[32,128,256]{2,1,0:T(8,128)(2,1)}, bf16[32,128,256]{2,1,0:T(8,128)(2,1)}, u32[]{:S(2)}, u32[]{:S(2)}) collective-permute-start(bf16[32,128,256]{2,1,0:T(8,128)(2,1)} %x_ref.3), channel_id=1, source_target_pairs={{0,1},{1,2},{2,3},{3,4},{4,5},{5,6},{6,7},{7,8},{8,9},{9,10},{10,1... | collective-permute-start | bytes 6291464 | tf_op jit(solution)/shard_map/ppermute | solution.py:242
  7.0 1.6 %copy-start = (bf16[32,128,256]{2,1,0:T(8,128)(2,1)S(1)}, bf16[32,128,256]{2,1,0:T(8,128)(2,1)}, u32[]{:S(2)}) copy-start(bf16[32,128,256]{2,1,0:T(8,128)(2,1)} %x_ref.3) | copy-start | bytes 6291460
  62.5 36.3 %copy-start.1 = (bf16[32,128,256]{2,1,0:T(8,128)(2,1)S(1)}, bf16[32,128,256]{2,1,0:T(8,128)(2,1)}, u32[]{:S(2)}) copy-start(bf16[32,128,256]{2,1,0:T(8,128)(2,1)} %x_ref.3) | copy-start | bytes 6291460
where the time goes:
time: 114 us
  Pallas kernels  105 us (92%)
  starting transfers between devices  5.59 us (5%)
  local copies, waits for them, and re-layouts  1.6 us (1%)
  between operations  1.36 us (1%)
    pallas_call x1, Pallas kernels, body(): call(functools.partial(reduce_kernel, n), jax.ShapeDtypeStruct(gram.shape...  50.8 us
    pallas_call x1, Pallas kernels, body(): call(whiten_kernel, [shape, shape], [SMEM, VMEM], [pltpu.VMEM((bands, ban...  36.2 us
    pallas_call x1, Pallas kernels, body(): call(score_kernel, jax.ShapeDtypeStruct((lines, cols), F32), [SMEM] + [VM...  14.9 us
    pallas_call x1, Pallas kernels, body(): call(gram_kernel, jax.ShapeDtypeStruct((4 * half, half), F32), [SMEM, VME...  3.21 us
    ppermute x1, starting transfers between devices, body(): before = lax.ppermute(pixels, 'lines', [(i, i + 1) for i in range(n - 1)])  3.02 us
    ppermute x1, starting transfers between devices, body(): after = lax.ppermute(pixels, 'lines', [(i + 1, i) for i in range(n - 1)])  2.57 us
  transfers between devices with their start and end apart: 2, of which 0 were waited for; matrix products, arithmetic and copies ran while one was open for 0% of the time, Pallas kernels for 79%

commit v1 on v0

--- a/solution.py
+++ b/solution.py
@@ -239,8 +239,6 @@
     n = lax.axis_size("lines")
     first = lax.axis_index("lines") * lines
     info = jnp.concatenate([first[None].astype(jnp.int32), scene_lines, scene_cols])
-    before = lax.ppermute(pixels, "lines", [(i, i + 1) for i in range(n - 1)])
-    after = lax.ppermute(pixels, "lines", [(i + 1, i) for i in range(n - 1)])
     half = bands // 2
     gram = call(
         gram_kernel, jax.ShapeDtypeStruct((4 * half, half), F32), [SMEM, VMEM],
@@ -252,7 +250,9 @@
         functools.partial(reduce_kernel, n), jax.ShapeDtypeStruct(gram.shape, F32), [VMEM],
         [pltpu.VMEM(gram.shape, F32)] + sems, 16, 4000000000, 40000000,
         collective_id=0, has_side_effects=True)(gram)
-    gram = gram.reshape(4 * half, half)
+    gram, halo = lax.optimization_barrier((gram.reshape(4 * half, half), pixels))
+    before = lax.ppermute(halo, "lines", [(i, i + 1) for i in range(n - 1)])
+    after = lax.ppermute(halo, "lines", [(i + 1, i) for i in range(n - 1)])
     shape = jax.ShapeDtypeStruct((bands, bands), BF16)
     high, low = call(
         whiten_kernel, [shape, shape], [SMEM, VMEM], [pltpu.VMEM((bands, bands), F32)], 16,

time: 114 us -> 89 us (0.78)
  Pallas kernels: 105 us -> 72.2 us
  waiting for transfers between devices: 0.01 us -> 8 us
    pallas_call x1, Pallas kernels: 50.8 us -> 18.9 us  [body(): call(functools.partial(reduce_kernel, n), jax.ShapeDtypeStruct(gram.shape...]
    ppermute x2, waiting for transfers between devices: 0.01 us -> 8 us  [the longest x1 7.99 us: body(): after = lax.ppermute(halo, 'lines', [(i + 1, i) for i in range(n - 1)])]
  transfers between devices with their start and end apart: 2 -> 2, of which waited for: 0 -> 1; matrix products, arithmetic and copies ran while one was open for 0% -> 0% of each run, Pallas kernels for 79% -> 41%
where the time goes in v1:
time: 89 us; the launch traced here: 88.8 us
  Pallas kernels  72.2 us (81%)
  waiting for transfers between devices  8 us (9%)
  starting transfers between devices  5.56 us (6%)
  local copies, waits for them, and re-layouts  1.6 us (2%)
  between operations  1.35 us (2%)
    pallas_call x1, Pallas kernels, body(): call(whiten_kernel, [shape, shape], [SMEM, VMEM], [pltpu.VMEM((bands, ban...  36.2 us
    pallas_call x1, Pallas kernels, body(): call(functools.partial(reduce_kernel, n), jax.ShapeDtypeStruct(gram.shape...  18.9 us
    pallas_call x1, Pallas kernels, body(): call(score_kernel, jax.ShapeDtypeStruct((lines, cols), F32), [SMEM] + [VM...  13.9 us
    ppermute x1, waiting for transfers between devices, body(): after = lax.ppermute(halo, 'lines', [(i + 1, i) for i in range(n - 1)])  7.99 us
    ppermute x1, starting transfers between devices, body(): before = lax.ppermute(halo, 'lines', [(i, i + 1) for i in range(n - 1)])  3.25 us
    pallas_call x1, Pallas kernels, body(): call(gram_kernel, jax.ShapeDtypeStruct((4 * half, half), F32), [SMEM, VME...  3.2 us
    ppermute x1, starting transfers between devices, body(): after = lax.ppermute(halo, 'lines', [(i + 1, i) for i in range(n - 1)])  2.31 us
  transfers between devices with their start and end apart: 2, of which 1 were waited for; matrix products, arithmetic and copies ran while one was open for 0% of the time, Pallas kernels for 41%

profile of v1, /device:TPU:29, one launch (start us, length us, event | category | flops | bytes accessed | tf_op | source)
XLA Modules:
  0.0 88.8 jit_solution(13666142644014570275)
XLA Ops:
  1.3 0.1 pad_add_fusion.info
  1.4 0.0 copy-start
  1.4 1.6 %copy-done = bf16[32,128,256]{2,1,0:T(8,128)(2,1)S(1)} copy-done((bf16[32,128,256]{2,1,0:T(8,128)(2,1)S(1)}, bf16[32,128,256]{2,1,0:T(8,128)(2,1)}, u32[]{:S(2)}) %copy-start) | copy-done | bytes 2097176
  3.0 3.2 %shard_map.37 = f32[512,128]{1,0:T(8,128)S(1)} custom-call(s32[3]{0:T(128)S(1)} %pad_add_fusion.info, bf16[32,128,256]{2,1,0:T(8,128)(2,1)S(1)} %copy-done), custom_call_target="tpu_custom_call" | custom-call | flops 4000000000 | bytes 2097152 | tf_op jit(solution)/shard_map/pallas_call | solution.py:243
  6.2 0.0 copy-start.1
  6.2 18.9 %shard_map.38 = f32[16,32,128]{2,1,0:T(8,128)S(1)} custom-call(f32[16,32,128]{2,1,0:T(8,128)S(1)} %bitcast.4), custom_call_target="tpu_custom_call" | custom-call | flops 4000000000 | bytes 40000000 | tf_op jit(solution)/shard_map/pallas_call | solution.py:249
  25.1 0.0 copy-done.1
  25.1 2.3 %collective-permute-start.1 = (bf16[32,128,256]{2,1,0:T(8,128)(2,1)S(1)}, bf16[32,128,256]{2,1,0:T(8,128)(2,1)S(1)}, u32[]{:S(2)}, u32[]{:S(2)}) collective-permute-start(bf16[32,128,256]{2,1,0:T(8,128)(2,1)S(1)} %copy-done.1), channel_id=1, source_target_pairs={{1,0},{2,1},{3,2},{4,3},{5,4},{6,5},{7,6},{8,7},{9,8},{10,9},{11,1... | collective-permute-start | bytes 6291464 | tf_op jit(solution)/shard_map/ppermute | solution.py:255
  27.4 3.3 %collective-permute-start = (bf16[32,128,256]{2,1,0:T(8,128)(2,1)S(1)}, bf16[32,128,256]{2,1,0:T(8,128)(2,1)S(1)}, u32[]{:S(2)}, u32[]{:S(2)}) collective-permute-start(bf16[32,128,256]{2,1,0:T(8,128)(2,1)S(1)} %copy-done.1), channel_id=1, source_target_pairs={{0,1},{1,2},{2,3},{3,4},{4,5},{5,6},{6,7},{7,8},{8,9},{9,10},{10,1... | collective-permute-start | bytes 6291464 | tf_op jit(solution)/shard_map/ppermute | solution.py:254
  30.7 36.2 %shard_map.39 = (bf16[256,256]{1,0:T(8,128)(2,1)S(1)}, bf16[256,256]{1,0:T(8,128)(2,1)S(1)}) custom-call(s32[3]{0:T(128)S(1)} %pad_add_fusion.info, f32[512,128]{1,0:T(8,128)S(1)} %bitcast.3), custom_call_target="tpu_custom_call" | custom-call | flops 10000000000 | bytes 60000000 | tf_op jit(solution)/shard_map/pallas_call | solution.py:257
  66.9 8.0 %collective-permute-done.1.after_ref = bf16[32,128,256]{2,1,0:T(8,128)(2,1)S(1)} collective-permute-done((bf16[32,128,256]{2,1,0:T(8,128)(2,1)S(1)}, bf16[32,128,256]{2,1,0:T(8,128)(2,1)S(1)}, u32[]{:S(2)}, u32[]{:S(2)}) %collective-permute-start.1) | collective-permute-done | bytes 2097184 | tf_op jit(solution)/shard_map/ppermute | solution.py:255
  74.9 0.0 collective-permute-done.before_ref
  74.9 13.9 %shard_map.40 = f32[32,128]{1,0:T(8,128)} custom-call(s32[3]{0:T(128)S(1)} %pad_add_fusion.info, bf16[32,128,256]{2,1,0:T(8,128)(2,1)S(1)} %copy-done.1, bf16[32,128,256]{2,1,0:T(8,128)(2,1)S(1)} %collective-permute-done.before_ref, bf16[32,128,256]{2,1,0:T(8,128)(2,1)S(1)} %collective-permute-done.1.after_ref, ...), custom_call_target="tpu_custom_call" | custom-call | flops 8000000000 | bytes 8000000 | tf_op jit(solution)/shard_map/pallas_call | solution.py:260
Async XLA Ops:
  1.4 1.6 %copy-start = (bf16[32,128,256]{2,1,0:T(8,128)(2,1)S(1)}, bf16[32,128,256]{2,1,0:T(8,128)(2,1)}, u32[]{:S(2)}) copy-start(bf16[32,128,256]{2,1,0:T(8,128)(2,1)} %x_ref.3) | copy-start | bytes 6291460
  6.2 18.9 %copy-start.1 = (bf16[32,128,256]{2,1,0:T(8,128)(2,1)S(1)}, bf16[32,128,256]{2,1,0:T(8,128)(2,1)}, u32[]{:S(2)}) copy-start(bf16[32,128,256]{2,1,0:T(8,128)(2,1)} %x_ref.3) | copy-start | bytes 6291460
  25.1 49.8 %collective-permute-start.1 = (bf16[32,128,256]{2,1,0:T(8,128)(2,1)S(1)}, bf16[32,128,256]{2,1,0:T(8,128)(2,1)S(1)}, u32[]{:S(2)}, u32[]{:S(2)}) collective-permute-start(bf16[32,128,256]{2,1,0:T(8,128)(2,1)S(1)} %copy-done.1), channel_id=1, source_target_pairs={{1,0},{2,1},{3,2},{4,3},{5,4},{6,5},{7,6},{8,7},{9,8},{10,9},{11,1... | collective-permute-start | bytes 6291464 | tf_op jit(solution)/shard_map/ppermute | solution.py:255
  27.4 47.5 %collective-permute-start = (bf16[32,128,256]{2,1,0:T(8,128)(2,1)S(1)}, bf16[32,128,256]{2,1,0:T(8,128)(2,1)S(1)}, u32[]{:S(2)}, u32[]{:S(2)}) collective-permute-start(bf16[32,128,256]{2,1,0:T(8,128)(2,1)S(1)} %copy-done.1), channel_id=1, source_target_pairs={{0,1},{1,2},{2,3},{3,4},{4,5},{5,6},{6,7},{7,8},{8,9},{9,10},{10,1... | collective-permute-start | bytes 6291464 | tf_op jit(solution)/shard_map/ppermute | solution.py:254

commit v2 on v1

--- a/solution.py
+++ b/solution.py
@@ -10,6 +10,8 @@
 OUTER = 32
 GUARD = 4
 SLAB = 32
+GROUP = 8
+EARLY = 8
 HIGHEST = lax.Precision.HIGHEST
 MESH = pl.DeviceIdType.MESH
 BF16 = jnp.bfloat16
@@ -129,16 +131,35 @@
     row = iota((SLAB, bands), 0)
     for base in range(0, bands, SLAB):
         slab = mat[base : base + SLAB, :]
-        pivots = jnp.ones((SLAB, bands), F32)
-        for j in range(SLAB):
-            k = base + j
-            column = jnp.broadcast_to(slab[:, k : k + 1], (SLAB, bands))
-            pivot = jnp.broadcast_to(column[j : j + 1, :], (SLAB, bands))
-            pivots = jnp.where(row == j, pivot, pivots)
-            factor = jnp.where(row > j, column / pivot, 0.0)
-            line = jnp.broadcast_to(slab[j : j + 1, :], (SLAB, bands))
-            line = jnp.where(lane == k, 1.0, line)
-            slab = jnp.where((lane == k) & (row > j), 0.0, slab) - factor * line
+        pivots = []
+        for top in range(0, SLAB, GROUP):
+            tail = slab[top:, :]
+            size = SLAB - top
+            narrow = iota((size, 128), 0)
+            wide_row = iota((size, bands), 0)
+            wide_lane = iota((size, bands), 1)
+            columns = [
+                jnp.broadcast_to(tail[:, k : k + 1], (size, 128))
+                for k in range(base + top, base + top + GROUP)
+            ]
+            group = jnp.ones((GROUP, 128), F32)
+            for j in range(GROUP):
+                k = base + top + j
+                pivot = jnp.broadcast_to(columns[j][j : j + 1, :], (GROUP, 128))
+                group = jnp.where(iota((GROUP, 128), 0) == j, pivot, group)
+                inverse = 1.0 / pivot
+                inverse = jnp.concatenate([inverse] * (size // GROUP), axis=0)
+                factor = jnp.where(narrow > j, columns[j] * inverse, 0.0)
+                for m in range(j + 1, GROUP):
+                    columns[m] = columns[m] - factor * jnp.broadcast_to(columns[m][j : j + 1, :], (size, 128))
+                line = jnp.where(wide_lane[:1] == k, 1.0, tail[j : j + 1, :])
+                keep = jnp.where((wide_lane == k) & (wide_row > j), 0.0, tail)
+                spread = jnp.concatenate([factor] * (bands // 128), axis=1)
+                tail = keep - spread * jnp.broadcast_to(line, (size, bands))
+            slab = jnp.concatenate([slab[:top, :], tail], axis=0) if top else tail
+            pivots.append(group)
+        pivots = jnp.concatenate(pivots, axis=0)
+        pivots = jnp.concatenate([pivots] * (bands // 128), axis=1)
         inside = (lane >= base) & (lane < base + SLAB)
         unit = jnp.where(lane == base + row, 1.0, jnp.where(inside & (lane > base + row), 0.0, slab))
         below = jnp.where(lane < base + SLAB, unit, 0.0)
@@ -155,19 +176,23 @@
             mat[base + SLAB :, :] = cleared - update[base + SLAB :, :]
 
 
-def score_kernel(info, x_ref, before_ref, after_ref, high_ref, low_ref, out_ref, ext, outer, guard):
+def score_kernel(info, x_ref, before_far, before_near, after_near, after_far, high_ref, low_ref, out_ref, ext, outer, guard):
     lines, cols, bands = x_ref.shape
     first, last_line, last_col = info[0], info[1], info[2]
     col_ok = iota((cols, bands), 0) < last_col
 
-    def mask(i, _):
-        for part, ref in enumerate((before_ref, x_ref, after_ref)):
-            line = first + (part - 1) * lines + i
+    start = 0
+    for ref in (before_far, before_near, x_ref, after_near, after_far):
+        count = ref.shape[0]
+
+        def mask(i, _, ref=ref, start=start):
+            line = first - lines + start + i
             ok = col_ok & (line >= 0) & (line < last_line)
-            ext[part * lines + i] = jnp.where(ok, ref[i].astype(F32), 0.0).astype(BF16)
-        return 0
-
-    lax.fori_loop(0, lines, mask, 0)
+            ext[start + i] = jnp.where(ok, ref[i].astype(F32), 0.0).astype(BF16)
+            return 0
+
+        lax.fori_loop(0, count, mask, 0)
+        start += count
 
     def total(lo, hi):
         def add(i, acc):
@@ -239,6 +264,10 @@
     n = lax.axis_size("lines")
     first = lax.axis_index("lines") * lines
     info = jnp.concatenate([first[None].astype(jnp.int32), scene_lines, scene_cols])
+    up = [(i, i + 1) for i in range(n - 1)]
+    down = [(i + 1, i) for i in range(n - 1)]
+    early_before = lax.ppermute(pixels[lines - EARLY :], "lines", up)
+    early_after = lax.ppermute(pixels[:EARLY], "lines", down)
     half = bands // 2
     gram = call(
         gram_kernel, jax.ShapeDtypeStruct((4 * half, half), F32), [SMEM, VMEM],
@@ -251,16 +280,16 @@
         [pltpu.VMEM(gram.shape, F32)] + sems, 16, 4000000000, 40000000,
         collective_id=0, has_side_effects=True)(gram)
     gram, halo = lax.optimization_barrier((gram.reshape(4 * half, half), pixels))
-    before = lax.ppermute(halo, "lines", [(i, i + 1) for i in range(n - 1)])
-    after = lax.ppermute(halo, "lines", [(i + 1, i) for i in range(n - 1)])
+    before = (lax.ppermute(halo[: lines - EARLY], "lines", up), early_before)
+    after = (early_after, lax.ppermute(halo[EARLY:], "lines", down))
     shape = jax.ShapeDtypeStruct((bands, bands), BF16)
     high, low = call(
         whiten_kernel, [shape, shape], [SMEM, VMEM], [pltpu.VMEM((bands, bands), F32)], 16,
         10000000000, 60000000)(info, gram)
     return call(
-        score_kernel, jax.ShapeDtypeStruct((lines, cols), F32), [SMEM] + [VMEM] * 5,
+        score_kernel, jax.ShapeDtypeStruct((lines, cols), F32), [SMEM] + [VMEM] * 7,
         [pltpu.VMEM((lines + 2 * OUTER, cols, bands), BF16)] + [pltpu.VMEM((cols, bands), F32)] * 2, 40,
-        8000000000, 8000000)(info, pixels, before, after, high, low)
+        8000000000, 8000000)(info, pixels, *before, *after, high, low)
 
 
 def solution(mesh):

time: 89 us -> 90.5 us (1.017)
  Pallas kernels: 72.2 us -> 47.6 us
  waiting for transfers between devices: 8 us -> 28.4 us
  starting transfers between devices: 5.56 us -> 10.7 us
    pallas_call x1, Pallas kernels: 36.2 us -> 11.2 us  [body(): call(whiten_kernel, [shape, shape], [SMEM, VMEM], [pltpu.VMEM((bands, ban...]
    ppermute x2 -> x4, waiting for transfers between devices: 8 us -> 28.4 us  [the longest x1 24.6 us: body(): early_after = lax.ppermute(pixels[:EARLY], 'lines', down)]
    ppermute x2 -> x4, starting transfers between devices: 5.56 us -> 10.7 us  [the longest x1 3.64 us: body(): early_before = lax.ppermute(pixels[lines - EARLY:], 'lines', up)]
  transfers between devices with their start and end apart: 2 -> 4, of which waited for: 1 -> 2; matrix products, arithmetic and copies ran while one was open for 0% -> 0% of each run, Pallas kernels for 41% -> 12%
where the time goes in v2:
time: 90.5 us; the launch traced here: 90.2 us
  Pallas kernels  47.6 us (53%)
  waiting for transfers between devices  28.4 us (31%)
  starting transfers between devices  10.7 us (12%)
  local copies, waits for them, and re-layouts  2.06 us (2%)
  between operations  1.38 us (2%)
    ppermute x1, waiting for transfers between devices, body(): early_after = lax.ppermute(pixels[:EARLY], 'lines', down)  24.6 us
    pallas_call x1, Pallas kernels, body(): call(functools.partial(reduce_kernel, n), jax.ShapeDtypeStruct(gram.shape...  18.9 us
    pallas_call x1, Pallas kernels, body(): call(score_kernel, jax.ShapeDtypeStruct((lines, cols), F32), [SMEM] + [VM...  14.3 us
    pallas_call x1, Pallas kernels, body(): call(whiten_kernel, [shape, shape], [SMEM, VMEM], [pltpu.VMEM((bands, ban...  11.2 us
    ppermute x1, waiting for transfers between devices, body(): early_before = lax.ppermute(pixels[lines - EARLY:], 'lines', up)  3.78 us
    ppermute x1, starting transfers between devices, body(): early_before = lax.ppermute(pixels[lines - EARLY:], 'lines', up)  3.64 us
    pallas_call x1, Pallas kernels, body(): call(gram_kernel, jax.ShapeDtypeStruct((4 * half, half), F32), [SMEM, VME...  3.2 us
    ppermute x1, starting transfers between devices, body(): before = (lax.ppermute(halo[:lines - EARLY], 'lines', up), early_before)  2.86 us
  transfers between devices with their start and end apart: 4, of which 2 were waited for; matrix products, arithmetic and copies ran while one was open for 0% of the time, Pallas kernels for 12%

profile of v2, /device:TPU:29, one launch (start us, length us, event | category | flops | bytes accessed | tf_op | source)
XLA Modules:
  0.0 90.2 jit_solution(9351444956085082775)
XLA Ops:
  1.3 0.1 pad_add_fusion.info
  1.4 0.0 copy-start
  1.4 1.6 %copy-done = bf16[32,128,256]{2,1,0:T(8,128)(2,1)S(1)} copy-done((bf16[32,128,256]{2,1,0:T(8,128)(2,1)S(1)}, bf16[32,128,256]{2,1,0:T(8,128)(2,1)}, u32[]{:S(2)}) %copy-start) | copy-done | bytes 2097176
  3.0 3.2 %shard_map.37 = f32[512,128]{1,0:T(8,128)S(1)} custom-call(s32[3]{0:T(128)S(1)} %pad_add_fusion.info, bf16[32,128,256]{2,1,0:T(8,128)(2,1)S(1)} %copy-done), custom_call_target="tpu_custom_call" | custom-call | flops 4000000000 | bytes 2097152 | tf_op jit(solution)/shard_map/pallas_call | solution.py:272
  6.2 0.0 copy-start.1
  6.2 18.9 %shard_map.38 = f32[16,32,128]{2,1,0:T(8,128)S(1)} custom-call(f32[16,32,128]{2,1,0:T(8,128)S(1)} %bitcast.4), custom_call_target="tpu_custom_call" | custom-call | flops 4000000000 | bytes 40000000 | tf_op jit(solution)/shard_map/pallas_call | solution.py:278
  25.1 0.0 copy-done.1
  25.1 0.4 fusion
  25.5 2.9 %collective-permute-start = (bf16[24,128,256]{2,1,0:T(8,128)(2,1)S(1)}, bf16[24,128,256]{2,1,0:T(8,128)(2,1)S(1)}, u32[]{:S(2)}, u32[]{:S(2)}) collective-permute-start(bf16[24,128,256]{2,1,0:T(8,128)(2,1)S(1)} %get-tuple-element.14), channel_id=1, source_target_pairs={{0,1},{1,2},{2,3},{3,4},{4,5},{5,6},{6,7},{7,8},{8,9},{9,10},{10,1... | collective-permute-start | bytes 4718600 | tf_op jit(solution)/shard_map/ppermute | solution.py:283
  28.4 1.9 %collective-permute-start.3 = (bf16[24,128,256]{2,1,0:T(8,128)(2,1)S(1)}, bf16[24,128,256]{2,1,0:T(8,128)(2,1)S(1)}, u32[]{:S(2)}, u32[]{:S(2)}) collective-permute-start(bf16[24,128,256]{2,1,0:T(8,128)(2,1)S(1)} %get-tuple-element.13), channel_id=1, source_target_pairs={{1,0},{2,1},{3,2},{4,3},{5,4},{6,5},{7,6},{8,7},{9,8},{10,9},{11,1... | collective-permute-start | bytes 4718600 | tf_op jit(solution)/shard_map/ppermute | solution.py:284
  30.3 0.1 fusion.1
  30.4 3.6 %collective-permute-start.1 = (bf16[8,128,256]{2,1,0:T(8,128)(2,1)S(1)}, bf16[8,128,256]{2,1,0:T(8,128)(2,1)S(1)}, u32[]{:S(2)}, u32[]{:S(2)}) collective-permute-start(bf16[8,128,256]{2,1,0:T(8,128)(2,1)S(1)} %get-tuple-element.16), channel_id=1, source_target_pairs={{0,1},{1,2},{2,3},{3,4},{4,5},{5,6},{6,7},{7,8},{8,9},{9,10},{10,1... | collective-permute-start | bytes 1572872 | tf_op jit(solution)/shard_map/ppermute | solution.py:269
  34.0 2.3 %collective-permute-start.2 = (bf16[8,128,256]{2,1,0:T(8,128)(2,1)S(1)}, bf16[8,128,256]{2,1,0:T(8,128)(2,1)S(1)}, u32[]{:S(2)}, u32[]{:S(2)}) collective-permute-start(bf16[8,128,256]{2,1,0:T(8,128)(2,1)S(1)} %get-tuple-element.15), channel_id=1, source_target_pairs={{1,0},{2,1},{3,2},{4,3},{5,4},{6,5},{7,6},{8,7},{9,8},{10,9},{11,1... | collective-permute-start | bytes 1572872 | tf_op jit(solution)/shard_map/ppermute | solution.py:270
  36.3 11.2 %shard_map.39 = (bf16[256,256]{1,0:T(8,128)(2,1)S(1)}, bf16[256,256]{1,0:T(8,128)(2,1)S(1)}) custom-call(s32[3]{0:T(128)S(1)} %pad_add_fusion.info, f32[512,128]{1,0:T(8,128)S(1)} %bitcast.3), custom_call_target="tpu_custom_call" | custom-call | flops 10000000000 | bytes 60000000 | tf_op jit(solution)/shard_map/pallas_call | solution.py:286
  47.5 3.8 %collective-permute-done.1.before_near = bf16[8,128,256]{2,1,0:T(8,128)(2,1)S(1)} collective-permute-done((bf16[8,128,256]{2,1,0:T(8,128)(2,1)S(1)}, bf16[8,128,256]{2,1,0:T(8,128)(2,1)S(1)}, u32[]{:S(2)}, u32[]{:S(2)}) %collective-permute-start.1) | collective-permute-done | bytes 524320 | tf_op jit(solution)/shard_map/ppermute | solution.py:269
  51.3 24.6 %collective-permute-done.2.after_near = bf16[8,128,256]{2,1,0:T(8,128)(2,1)S(1)} collective-permute-done((bf16[8,128,256]{2,1,0:T(8,128)(2,1)S(1)}, bf16[8,128,256]{2,1,0:T(8,128)(2,1)S(1)}, u32[]{:S(2)}, u32[]{:S(2)}) %collective-permute-start.2) | collective-permute-done | bytes 524320 | tf_op jit(solution)/shard_map/ppermute | solution.py:270
  75.9 0.0 collective-permute-done.before_far
  75.9 0.0 collective-permute-done.3.after_far
  75.9 14.3 %shard_map.40 = f32[32,128]{1,0:T(8,128)} custom-call(s32[3]{0:T(128)S(1)} %pad_add_fusion.info, bf16[32,128,256]{2,1,0:T(8,128)(2,1)S(1)} %copy-done.1, bf16[24,128,256]{2,1,0:T(8,128)(2,1)S(1)} %collective-permute-done.before_far, bf16[8,128,256]{2,1,0:T(8,128)(2,1)S(1)} %collective-permute-done.1.before_near, ...), custom_call_target="tpu_custom_call" | custom-call | flops 8000000000 | bytes 8000000 | tf_op jit(solution)/shard_map/pallas_call | solution.py:289
Async XLA Ops:
  1.4 1.6 %copy-start = (bf16[32,128,256]{2,1,0:T(8,128)(2,1)S(1)}, bf16[32,128,256]{2,1,0:T(8,128)(2,1)}, u32[]{:S(2)}) copy-start(bf16[32,128,256]{2,1,0:T(8,128)(2,1)} %x_ref.3) | copy-start | bytes 6291460
  6.2 18.9 %copy-start.1 = (bf16[32,128,256]{2,1,0:T(8,128)(2,1)S(1)}, bf16[32,128,256]{2,1,0:T(8,128)(2,1)}, u32[]{:S(2)}) copy-start(bf16[32,128,256]{2,1,0:T(8,128)(2,1)} %x_ref.3) | copy-start | bytes 6291460
  25.5 50.4 %collective-permute-start = (bf16[24,128,256]{2,1,0:T(8,128)(2,1)S(1)}, bf16[24,128,256]{2,1,0:T(8,128)(2,1)S(1)}, u32[]{:S(2)}, u32[]{:S(2)}) collective-permute-start(bf16[24,128,256]{2,1,0:T(8,128)(2,1)S(1)} %get-tuple-element.14), channel_id=1, source_target_pairs={{0,1},{1,2},{2,3},{3,4},{4,5},{5,6},{6,7},{7,8},{8,9},{9,10},{10,1... | collective-permute-start | bytes 4718600 | tf_op jit(solution)/shard_map/ppermute | solution.py:283
  28.4 47.6 %collective-permute-start.3 = (bf16[24,128,256]{2,1,0:T(8,128)(2,1)S(1)}, bf16[24,128,256]{2,1,0:T(8,128)(2,1)S(1)}, u32[]{:S(2)}, u32[]{:S(2)}) collective-permute-start(bf16[24,128,256]{2,1,0:T(8,128)(2,1)S(1)} %get-tuple-element.13), channel_id=1, source_target_pairs={{1,0},{2,1},{3,2},{4,3},{5,4},{6,5},{7,6},{8,7},{9,8},{10,9},{11,1... | collective-permute-start | bytes 4718600 | tf_op jit(solution)/shard_map/ppermute | solution.py:284
  30.4 20.9 %collective-permute-start.1 = (bf16[8,128,256]{2,1,0:T(8,128)(2,1)S(1)}, bf16[8,128,256]{2,1,0:T(8,128)(2,1)S(1)}, u32[]{:S(2)}, u32[]{:S(2)}) collective-permute-start(bf16[8,128,256]{2,1,0:T(8,128)(2,1)S(1)} %get-tuple-element.16), channel_id=1, source_target_pairs={{0,1},{1,2},{2,3},{3,4},{4,5},{5,6},{6,7},{7,8},{8,9},{9,10},{10,1... | collective-permute-start | bytes 1572872 | tf_op jit(solution)/shard_map/ppermute | solution.py:269
  34.0 41.9 %collective-permute-start.2 = (bf16[8,128,256]{2,1,0:T(8,128)(2,1)S(1)}, bf16[8,128,256]{2,1,0:T(8,128)(2,1)S(1)}, u32[]{:S(2)}, u32[]{:S(2)}) collective-permute-start(bf16[8,128,256]{2,1,0:T(8,128)(2,1)S(1)} %get-tuple-element.15), channel_id=1, source_target_pairs={{1,0},{2,1},{3,2},{4,3},{5,4},{6,5},{7,6},{8,7},{9,8},{10,9},{11,1... | collective-permute-start | bytes 1572872 | tf_op jit(solution)/shard_map/ppermute | solution.py:270

commit v3 on v2

--- a/solution.py
+++ b/solution.py
@@ -12,6 +12,7 @@
 SLAB = 32
 GROUP = 8
 EARLY = 8
+CHUNK = 4
 HIGHEST = lax.Precision.HIGHEST
 MESH = pl.DeviceIdType.MESH
 BF16 = jnp.bfloat16
@@ -59,8 +60,19 @@
     out_ref[3 * h + 8 : 3 * h + 16] = sums[:, h:]
 
 
-def reduce_kernel(n, g_ref, out_ref, recv, s1, r1, s2, r2):
+def halo(source, target, send, recv, index, peer):
+    return pltpu.make_async_remote_copy(
+        src_ref=source, dst_ref=target, send_sem=send.at[index], recv_sem=recv.at[index],
+        device_id={"lines": peer}, device_id_type=MESH)
+
+
+def reduce_kernel(n, g_ref, x_ref, out_ref, before_ref, after_ref, recv, s1, r1, s2, r2, s3, r3):
     me = lax.axis_index("lines")
+    lines = x_ref.shape[0]
+    has_left, has_right = me > 0, me < n - 1
+    left, right = lax.rem(me + n - 1, n), lax.rem(me + 1, n)
+    near = x_ref.at[pl.ds(lines - EARLY, EARLY)]
+    lead = x_ref.at[pl.ds(0, EARLY)]
     bar = pltpu.get_barrier_semaphore()
 
     def greet(d, _):
@@ -87,6 +99,14 @@
         return 0
 
     lax.fori_loop(1, n, start1, 0)
+
+    @pl.when(has_right)
+    def _():
+        halo(near, before_ref, s3, r3, 0, right).start()
+
+    @pl.when(has_left)
+    def _():
+        halo(lead, after_ref, s3, r3, 1, left).start()
 
     def take(d, total):
         source = lax.rem(me + n - d, n)
@@ -114,8 +134,18 @@
 
     lax.fori_loop(1, n, finish, 0)
 
-
-def whiten_kernel(info, g_ref, high_ref, low_ref, mat):
+    @pl.when(has_right)
+    def _():
+        halo(near, before_ref, s3, r3, 0, right).wait_send()
+        halo(lead, after_ref, s3, r3, 1, right).wait_recv()
+
+    @pl.when(has_left)
+    def _():
+        halo(lead, after_ref, s3, r3, 1, left).wait_send()
+        halo(near, before_ref, s3, r3, 0, left).wait_recv()
+
+
+def whiten_part(info, g_ref, high_ref, low_ref, mat):
     h = g_ref.shape[1]
     bands = 2 * h
     total = (info[1] * info[2]).astype(F32)
@@ -176,31 +206,71 @@
             mat[base + SLAB :, :] = cleared - update[base + SLAB :, :]
 
 
-def score_kernel(info, x_ref, before_far, before_near, after_near, after_far, high_ref, low_ref, out_ref, ext, outer, guard):
+def score_kernel(n, info, g_ref, x_ref, near_before, near_after, out_ref, far_before, far_after,
+                 high_ref, low_ref, mat, ext, outer_f, guard_f, outer_b, guard_b, send, recv):
     lines, cols, bands = x_ref.shape
+    far = lines - EARLY
+    chunks = far // CHUNK
+    me = lax.axis_index("lines")
+    has_left, has_right = me > 0, me < n - 1
+    left, right = lax.rem(me + n - 1, n), lax.rem(me + 1, n)
+    bar = pltpu.get_barrier_semaphore()
+
+    @pl.when(has_left)
+    def _():
+        pl.semaphore_signal(bar, inc=1, device_id={"lines": left}, device_id_type=MESH)
+
+    @pl.when(has_right)
+    def _():
+        pl.semaphore_signal(bar, inc=1, device_id={"lines": right}, device_id_type=MESH)
+
+    pl.semaphore_wait(bar, has_left.astype(jnp.int32) + has_right.astype(jnp.int32))
+
+    def copy_before(m, peer):
+        rows = pl.ds(far - (m + 1) * CHUNK, CHUNK)
+        return halo(x_ref.at[rows], far_before.at[rows], send, recv, m, peer)
+
+    def copy_after(m, peer):
+        return halo(x_ref.at[pl.ds(EARLY + m * CHUNK, CHUNK)], far_after.at[pl.ds(m * CHUNK, CHUNK)],
+                    send, recv, chunks + m, peer)
+
+    for m in range(chunks):
+        @pl.when(has_right)
+        def _():
+            copy_before(m, right).start()
+
+        @pl.when(has_left)
+        def _():
+            copy_after(m, left).start()
+
+    whiten_part(info, g_ref, high_ref, low_ref, mat)
+
     first, last_line, last_col = info[0], info[1], info[2]
     col_ok = iota((cols, bands), 0) < last_col
 
-    start = 0
-    for ref in (before_far, before_near, x_ref, after_near, after_far):
-        count = ref.shape[0]
-
-        def mask(i, _, ref=ref, start=start):
+    def mask(ref, source, start, count):
+        def one(i, _):
             line = first - lines + start + i
             ok = col_ok & (line >= 0) & (line < last_line)
-            ext[start + i] = jnp.where(ok, ref[i].astype(F32), 0.0).astype(BF16)
+            ext[start + i] = jnp.where(ok, ref[source + i].astype(F32), 0.0).astype(BF16)
             return 0
-
-        lax.fori_loop(0, count, mask, 0)
-        start += count
-
-    def total(lo, hi):
+        lax.fori_loop(0, count, one, 0)
+
+    mask(near_before, 0, far, EARLY)
+    mask(x_ref, 0, lines, lines)
+    mask(near_after, 0, 2 * lines, EARLY)
+
+    def total(lo, hi, acc):
         def add(i, acc):
             return acc + ext[i].astype(F32)
-        return lax.fori_loop(lo, hi, add, jnp.zeros((cols, bands), F32))
-
-    outer[...] = total(lines - OUTER, lines + OUTER)
-    guard[...] = total(lines - GUARD, lines + GUARD)
+        return lax.fori_loop(lo, hi, add, acc)
+
+    half = lines // 2
+    zero = jnp.zeros((cols, bands), F32)
+    guard_f[...] = total(lines + half - GUARD, lines + half + GUARD, zero)
+    guard_b[...] = guard_f[...]
+    outer_f[...] = total(far, 2 * lines + EARLY, zero)
+
     gap = jnp.abs(iota((cols, cols), 0) - iota((cols, cols), 1))
     near = jnp.where(gap <= OUTER, 1.0, 0.0).astype(BF16)
     close = jnp.where(gap <= GUARD, -1.0, 0.0).astype(BF16)
@@ -212,39 +282,77 @@
 
     outer_cols = span(col, last_col, OUTER).astype(F32)
     guard_cols = span(col, last_col, GUARD).astype(F32)
-    step = 2
-
-    def score(i, _):
-        highs, lows = [], []
-        for j in range(step):
-            line = i * step + j
-            at = lines + line
-            wide = outer[...] + ext[at + OUTER].astype(F32)
-            tight = guard[...] + ext[at + GUARD].astype(F32)
-            stack = jnp.concatenate(split(wide) + split(tight), axis=0)
-            outer[...] = wide - ext[at - OUTER].astype(F32)
-            guard[...] = tight - ext[at - GUARD].astype(F32)
-            cycle = jnp.dot(windows, stack, preferred_element_type=F32)
-            place = first + line
-            count = (span(place, last_line, OUTER).astype(F32) * outer_cols
-                     - span(place, last_line, GUARD).astype(F32) * guard_cols)
-            deviation = x_ref[line].astype(F32) - cycle / jnp.maximum(count, 1.0)
-            high, low = split(deviation)
-            highs.append(high)
-            lows.append(low)
-        high = jnp.concatenate(highs, axis=0)
-        low = jnp.concatenate(lows, axis=0)
-        white = lax.dot_general(high_ref[...], high, NT, preferred_element_type=F32)
-        white += lax.dot_general(high_ref[...], low, NT, preferred_element_type=F32)
-        white += lax.dot_general(low_ref[...], high, NT, preferred_element_type=F32)
-        power = jnp.sum(white * white, axis=0, keepdims=True) / bands
-        for j in range(step):
-            line = i * step + j
-            ok = (iota((1, cols), 1) < last_col) & (first + line < last_line)
-            out_ref[pl.ds(line, 1), :] = jnp.where(ok, power[:, j * cols : (j + 1) * cols], 0.0)
-        return 0
-
-    lax.fori_loop(0, lines // step, score, 0)
+
+    def deviate(line, wide, tight):
+        stack = jnp.concatenate(split(wide) + split(tight), axis=0)
+        cycle = jnp.dot(windows, stack, preferred_element_type=F32)
+        place = first + line
+        count = (span(place, last_line, OUTER).astype(F32) * outer_cols
+                 - span(place, last_line, GUARD).astype(F32) * guard_cols)
+        return split(x_ref[line].astype(F32) - cycle / jnp.maximum(count, 1.0))
+
+    def score(base):
+        def one(i, _):
+            places, parts = [], []
+            for j in range(2):
+                line = half + base + i * 2 + j
+                at = lines + line
+                wide = outer_f[...] + ext[at + OUTER].astype(F32)
+                tight = guard_f[...] + ext[at + GUARD].astype(F32)
+                outer_f[...] = wide - ext[at - OUTER].astype(F32)
+                guard_f[...] = tight - ext[at - GUARD].astype(F32)
+                places.append(line)
+                parts.append(deviate(line, wide, tight))
+                line = half - 1 - base - i * 2 - j
+                at = lines + line
+                wide = outer_b[...] + ext[at - OUTER].astype(F32)
+                tight = guard_b[...] + ext[at - GUARD].astype(F32)
+                outer_b[...] = wide - ext[at + OUTER].astype(F32)
+                guard_b[...] = tight - ext[at + GUARD].astype(F32)
+                places.append(line)
+                parts.append(deviate(line, wide, tight))
+            high = jnp.concatenate([p[0] for p in parts], axis=0)
+            low = jnp.concatenate([p[1] for p in parts], axis=0)
+            white = lax.dot_general(high_ref[...], high, NT, preferred_element_type=F32)
+            white += lax.dot_general(high_ref[...], low, NT, preferred_element_type=F32)
+            white += lax.dot_general(low_ref[...], high, NT, preferred_element_type=F32)
+            power = jnp.sum(white * white, axis=0, keepdims=True) / bands
+            for j, line in enumerate(places):
+                ok = (iota((1, cols), 1) < last_col) & (first + line < last_line)
+                out_ref[pl.ds(line, 1), :] = jnp.where(ok, power[:, j * cols : (j + 1) * cols], 0.0)
+            return 0
+        lax.fori_loop(0, CHUNK // 2, one, 0)
+
+    ready = (half - EARLY) // CHUNK
+    for m in range(chunks):
+        @pl.when(has_left)
+        def _():
+            copy_before(m, left).wait_recv()
+
+        @pl.when(has_right)
+        def _():
+            copy_after(m, right).wait_recv()
+
+        lo = far - (m + 1) * CHUNK
+        hi = m * CHUNK
+        mask(far_before, lo, lo, CHUNK)
+        mask(far_after, hi, 2 * lines + EARLY + hi, CHUNK)
+        if m < ready:
+            acc = total(lo, lo + CHUNK, outer_f[...])
+            outer_f[...] = total(2 * lines + EARLY + hi, 2 * lines + EARLY + hi + CHUNK, acc)
+            if m == ready - 1:
+                outer_b[...] = outer_f[...]
+        else:
+            score((m - ready) * CHUNK)
+
+    for m in range(chunks):
+        @pl.when(has_right)
+        def _():
+            copy_before(m, right).wait_send()
+
+        @pl.when(has_left)
+        def _():
+            copy_after(m, left).wait_send()
 
 
 VMEM = pl.BlockSpec(memory_space=pltpu.VMEM)
@@ -264,10 +372,6 @@
     n = lax.axis_size("lines")
     first = lax.axis_index("lines") * lines
     info = jnp.concatenate([first[None].astype(jnp.int32), scene_lines, scene_cols])
-    up = [(i, i + 1) for i in range(n - 1)]
-    down = [(i + 1, i) for i in range(n - 1)]
-    early_before = lax.ppermute(pixels[lines - EARLY :], "lines", up)
-    early_after = lax.ppermute(pixels[:EARLY], "lines", down)
     half = bands // 2
     gram = call(
         gram_kernel, jax.ShapeDtypeStruct((4 * half, half), F32), [SMEM, VMEM],
@@ -275,21 +379,22 @@
         4000000000, pixels.size * 2)(info, pixels)
     gram = gram.reshape(n, 4 * half // n, half)
     sems = [pltpu.SemaphoreType.DMA((n,))] * 4
-    gram = call(
-        functools.partial(reduce_kernel, n), jax.ShapeDtypeStruct(gram.shape, F32), [VMEM],
-        [pltpu.VMEM(gram.shape, F32)] + sems, 16, 4000000000, 40000000,
-        collective_id=0, has_side_effects=True)(gram)
-    gram, halo = lax.optimization_barrier((gram.reshape(4 * half, half), pixels))
-    before = (lax.ppermute(halo[: lines - EARLY], "lines", up), early_before)
-    after = (early_after, lax.ppermute(halo[EARLY:], "lines", down))
-    shape = jax.ShapeDtypeStruct((bands, bands), BF16)
-    high, low = call(
-        whiten_kernel, [shape, shape], [SMEM, VMEM], [pltpu.VMEM((bands, bands), F32)], 16,
-        10000000000, 60000000)(info, gram)
+    edge = jax.ShapeDtypeStruct((EARLY, cols, bands), BF16)
+    gram, before, after = call(
+        functools.partial(reduce_kernel, n), [jax.ShapeDtypeStruct(gram.shape, F32), edge, edge], [VMEM, VMEM],
+        [pltpu.VMEM(gram.shape, F32)] + sems + [pltpu.SemaphoreType.DMA((2,))] * 2, 32, 4000000000, 40000000,
+        collective_id=0, has_side_effects=True)(gram, pixels)
+    gram = gram.reshape(4 * half, half)
+    far = lines - EARLY
+    pieces = pltpu.SemaphoreType.DMA((2 * (far // CHUNK),))
+    scratch = (
+        [pltpu.VMEM((far, cols, bands), BF16)] * 2 + [pltpu.VMEM((bands, bands), BF16)] * 2
+        + [pltpu.VMEM((bands, bands), F32), pltpu.VMEM((lines + 2 * OUTER, cols, bands), BF16)]
+        + [pltpu.VMEM((cols, bands), F32)] * 4 + [pieces] * 2)
     return call(
-        score_kernel, jax.ShapeDtypeStruct((lines, cols), F32), [SMEM] + [VMEM] * 7,
-        [pltpu.VMEM((lines + 2 * OUTER, cols, bands), BF16)] + [pltpu.VMEM((cols, bands), F32)] * 2, 40,
-        8000000000, 8000000)(info, pixels, *before, *after, high, low)
+        functools.partial(score_kernel, n), jax.ShapeDtypeStruct((lines, cols), F32), [SMEM] + [VMEM] * 4,
+        scratch, 48, 8000000000, 80000000, collective_id=1, has_side_effects=True)(
+            info, gram, pixels, before, after)
 
 
 def solution(mesh):

time: 90.5 us -> 69.9 us (0.77); the launches traced: 90.2 us -> 68.6 us
  waiting for transfers between devices: 28.4 us -> 0 us
  Pallas kernels: 47.6 us -> 65 us
  starting transfers between devices: 10.7 us -> 0 us
    ppermute x4 -> x0, waiting for transfers between devices: 28.4 us -> none  [the longest x1 24.6 us: body(): early_after = lax.ppermute(pixels[:EARLY], 'lines', down)]
    pallas_call x3 -> x2, Pallas kernels: 44.4 us -> 61.8 us  [the longest x1 39.4 us: body(): call(functools.partial(score_kernel, n), jax.ShapeDtypeStruct((lines, col...]
    ppermute x4 -> x0, starting transfers between devices: 10.7 us -> none  [the longest x1 3.64 us: body(): early_before = lax.ppermute(pixels[lines - EARLY:], 'lines', up)]
    unnamed x4 -> x5, local copies, waits for them, and re-layouts: 1.6 us -> 2.2 us
  transfers between devices with their start and end apart: 4 -> 0, of which waited for: 2 -> 0; matrix products, arithmetic and copies ran while one was open for 0% -> 0% of each run, Pallas kernels for 12% -> 0%
where the time goes in v3:
time: 69.9 us; the launch traced here: 68.6 us
  Pallas kernels  65 us (93%)
  local copies, waits for them, and re-layouts  2.2 us (3%)
  between operations  1.33 us (2%)
    pallas_call x1, Pallas kernels, body(): call(functools.partial(score_kernel, n), jax.ShapeDtypeStruct((lines, col...  39.4 us
    pallas_call x1, Pallas kernels, body(): call(functools.partial(reduce_kernel, n), [jax.ShapeDtypeStruct(gram.shap...  22.3 us
    pallas_call x1, Pallas kernels, body(): call(gram_kernel, jax.ShapeDtypeStruct((4 * half, half), F32), [SMEM, VME...  3.2 us
    unnamed x5, local copies, waits for them, and re-layouts  2.2 us

profile of v3, /device:TPU:29, one launch (start us, length us, event | category | flops | bytes accessed | tf_op | source)
XLA Modules:
  0.0 68.6 jit_solution(17738833557177272418)
XLA Ops:
  1.3 0.1 pad_add_fusion.info
  1.4 0.0 copy-start
  1.4 1.6 %copy-done = bf16[32,128,256]{2,1,0:T(8,128)(2,1)S(1)} copy-done((bf16[32,128,256]{2,1,0:T(8,128)(2,1)S(1)}, bf16[32,128,256]{2,1,0:T(8,128)(2,1)}, u32[]{:S(2)}) %copy-start) | copy-done | bytes 2097176
  3.0 0.0 copy-start.1
  3.0 3.2 %shard_map.37 = f32[512,128]{1,0:T(8,128)S(1)} custom-call(s32[3]{0:T(128)S(1)} %pad_add_fusion.info, bf16[32,128,256]{2,1,0:T(8,128)(2,1)S(1)} %copy-done), custom_call_target="tpu_custom_call" | custom-call | flops 4000000000 | bytes 2097152 | tf_op jit(solution)/shard_map/pallas_call | solution.py:376
  6.2 0.0 copy-done.1
  6.2 22.3 %shard_map.38 = (f32[16,32,128]{2,1,0:T(8,128)S(1)}, bf16[8,128,256]{2,1,0:T(8,128)(2,1)S(1)}, bf16[8,128,256]{2,1,0:T(8,128)(2,1)S(1)}) custom-call(f32[16,32,128]{2,1,0:T(8,128)S(1)} %bitcast.4, bf16[32,128,256]{2,1,0:T(8,128)(2,1)S(1)} %copy-done.1), custom_call_target="tpu_custom_call" | custom-call | flops 4000000000 | bytes 40000000 | tf_op jit(solution)/shard_map/pallas_call | solution.py:383
  28.5 39.4 %shard_map.39 = f32[32,128]{1,0:T(8,128)S(1)} custom-call(s32[3]{0:T(128)S(1)} %pad_add_fusion.info, f32[512,128]{1,0:T(8,128)S(1)} %bitcast.3, bf16[32,128,256]{2,1,0:T(8,128)(2,1)S(1)} %copy-done.1, bf16[8,128,256]{2,1,0:T(8,128)(2,1)S(1)} %get-tuple-element.9.near_before, bf16[8,128,256]{2,1,0:T(8,128)(2,1)S(1)} %get-tuple-element.10.near_after), custom_call_target="tpu_custom_call" | custom-call | flops 8000000000 | bytes 80000000 | tf_op jit(solution)/shard_map/pallas_call | solution.py:394
  68.0 0.6 copy.7
Async XLA Ops:
  1.4 1.6 %copy-start = (bf16[32,128,256]{2,1,0:T(8,128)(2,1)S(1)}, bf16[32,128,256]{2,1,0:T(8,128)(2,1)}, u32[]{:S(2)}) copy-start(bf16[32,128,256]{2,1,0:T(8,128)(2,1)} %x_ref.5) | copy-start | bytes 6291460
  3.0 3.2 %copy-start.1 = (bf16[32,128,256]{2,1,0:T(8,128)(2,1)S(1)}, bf16[32,128,256]{2,1,0:T(8,128)(2,1)}, u32[]{:S(2)}) copy-start(bf16[32,128,256]{2,1,0:T(8,128)(2,1)} %x_ref.5) | copy-start | bytes 6291460
